TPU v7x, 512 devices: a whole 4x8x8 slice. The times are simulated.
512 devices in a mesh: row: 8 (over z), col: 16 (over y_hi, x, core), kpart: 4 (over y_lo).
Axes of the slice: x: 4, y: 8 (y_hi: 2, y_lo: 4; y = y_hi * 4 + y_lo), z: 8, core: 2. Of those that a mesh axis runs over, the one named last changes fastest.
Arguments:
- left_cyclic: float32 [2048, 8192], P(('kpart', 'col'), 'row'), may hold values from -6 to 6
- right_cyclic: float32 [2048, 16384], P(('kpart', 'row'), 'col'), may hold values from -0.125 to 0.125
Outputs:
- product: float32 [8192, 16384], P(('row', 'kpart'), 'col')
All inputs are finite; a program needn't handle non-finite values.
Results may differ from a plain program's by a relative error of at most 0.00007.
Values sent between devices are 32-bit elements; how exact they have to be, the bound alone decides.
No kernel may reach another device: no remote copies, remote signals or barrier semaphores. Data moves between devices by JAX's collectives and lax.ppermute only.
A program may use at most 64 MiB of HBM per device.

v0:
```python
import jax
import jax.numpy as jnp
from jax import lax
from jax.sharding import PartitionSpec as P

NB = 64


def contract(left_part, right_part):
    return lax.dot_general(
        left_part,
        right_part,
        (((0,), (0,)), ((), ())),
        precision=lax.Precision.HIGHEST,
        preferred_element_type=jnp.float32,
    )


def shards(left_cyclic, right_cyclic):
    row_count = lax.axis_size("row")
    column_count = lax.axis_size("col")
    slab_left, local_rows = left_cyclic.shape
    group_left = local_rows // (NB * row_count)
    shaped_left = left_cyclic.reshape(slab_left, row_count, group_left, 1, NB)
    moved_left = lax.all_to_all(shaped_left, "row", split_axis=1, concat_axis=3, tiled=True)
    band_left = moved_left.reshape(slab_left, local_rows)
    left_band = lax.all_gather(band_left, "col", axis=0, tiled=True)
    slab_right, local_cols = right_cyclic.shape
    group_right = local_cols // (NB * column_count)
    shaped_right = right_cyclic.reshape(slab_right, column_count, group_right, 1, NB)
    moved_right = lax.all_to_all(shaped_right, "col", split_axis=1, concat_axis=3, tiled=True)
    band_right = moved_right.reshape(slab_right, local_cols)
    right_band = lax.all_gather(band_right, "row", axis=0, tiled=True)
    return lax.psum_scatter(
        contract(left_band, right_band), "kpart", scatter_dimension=0, tiled=True
    )


def solution(mesh):
    placed = (P(("kpart", "col"), "row"), P(("kpart", "row"), "col"))
    return jax.shard_map(
        shards, mesh=mesh, in_specs=placed, out_specs=P(("row", "kpart"), "col"), check_vma=False
    )
```

profile of v0, /device:TPU:57, one launch (start us, length us, event | category | flops | bytes accessed | tf_op | source)
XLA Modules:
  0.0 246.7 jit_solution(4141008044242358849)
XLA Ops:
  6.5 0.0 all-gather.5.cloned.1.call-start
  6.5 1.1 reshape.19
  7.6 0.2 copy.11
  7.8 0.3 reshape.23
  8.1 0.0 copy-start
  8.2 16.5 %all_to_all.24 = f32[16,1,4096]{2,1,0:T(1,128)S(1)} all-to-all(f32[16,1,4096]{2,1,0:T(1,128)S(1)} %reshape.23), channel_id=1, replica_groups=mesh['row'=8,'col'=16,'kpart'=4] {'col'}, dimensions={0} | all-to-all | bytes 524288 | tf_op jit(solution)/shard_map/all_to_all | solution.py:31
  24.7 0.5 broadcast
  25.2 1.2 reduce.1
  26.5 0.2 reshape.24
  26.7 0.3 copy.8
  27.0 0.9 reshape.20
  27.9 0.0 all-gather.5.cloned.1.call-update
  27.9 0.0 all-gather.3.cloned.1.call-start
  28.0 0.0 copy-done
  28.0 0.2 reshape.17
  28.2 0.1 copy.12
  28.3 0.3 reshape.21
  28.5 17.6 %all_to_all.25 = f32[8,1,4096]{2,1,0:T(1,128)S(1)} all-to-all(f32[8,1,4096]{2,1,0:T(1,128)S(1)} %reshape.21), channel_id=1, replica_groups=mesh['row'=8,'col'=16,'kpart'=4] {'row'}, dimensions={0} | all-to-all | bytes 262144 | tf_op jit(solution)/shard_map/all_to_all | solution.py:25
  46.1 0.9 reduce
  47.1 0.2 reshape.22
  47.3 0.2 copy.6
  47.5 0.8 reshape.18
  48.2 0.0 all-gather.3.cloned.1.call-update
  48.3 0.0 reduce-scatter.2.cloned.1.call-start
  48.3 25.2 %all-gather.5.cloned.1.call-done = f32[512,1024]{1,0:T(8,128)} async-done(((f32[64,1024]{1,0:T(8,128)}), f32[512,1024]{1,0:T(8,128)}) %all-gather.5.cloned.1.call-update) | async-done | bytes 2097168 | tf_op jit(solution)/shard_map/all_gather | solution.py:33
  73.5 68.3 %all-gather.3.cloned.1.call-done = f32[512,1024]{1,0:T(8,128)} async-done(((f32[32,1024]{1,0:T(8,128)}), f32[512,1024]{1,0:T(8,128)}) %all-gather.3.cloned.1.call-update) | async-done | bytes 2097168 | tf_op jit(solution)/shard_map/all_gather | solution.py:27
  141.8 10.2 %fusion = f32[1024,1024]{1,0:T(8,128)} fusion(f32[512,1024]{1,0:T(8,128)} %all-gather.3.cloned.1.call-done, f32[512,1024]{1,0:T(8,128)} %all-gather.5.cloned.1.call-done), kind=kOutput, calls=%fused_computation.3 | convolution fusion | flops 6442450944 | bytes 8388608 | tf_op jit(solution)/shard_map/dot_general | solution.py:10
  152.0 0.0 reduce-scatter.2.cloned.1.call-update
  152.0 88.2 %reduce-scatter.2.cloned.1.call-done = f32[256,1024]{1,0:T(8,128)} async-done(((f32[1024,1024]{1,0:T(8,128)}), f32[256,1024]{1,0:T(8,128)}) %reduce-scatter.2.cloned.1.call-update) | async-done | bytes 1048592 | tf_op jit(solution)/shard_map/reduce_scatter | solution.py:34
  (1 shorter events, 0.0 us)
Async XLA Ops:
  6.5 66.9 %all-gather.5.cloned.1.call-start = ((), (), s32[]{:S(2)}) async-start(), calls=%async_computation.4 | async-start | bytes 2359296 | tf_op jit(solution)/shard_map/all_gather | solution.py:33
  8.1 19.8 %copy-start = (f32[32,1024]{1,0:T(8,128)S(1)}, f32[32,1024]{1,0:T(8,128)}, u32[]{:S(2)}) copy-start(f32[32,1024]{1,0:T(8,128)} %param.2) | copy-start | bytes 393220
  27.9 113.9 %all-gather.3.cloned.1.call-start = ((), (), s32[]{:S(2)}) async-start(), calls=%async_computation.3 | async-start | bytes 2228224 | tf_op jit(solution)/shard_map/all_gather | solution.py:27
  48.3 191.9 %reduce-scatter.2.cloned.1.call-start = ((), (), s32[]{:S(2)}) async-start(), calls=%async_computation.5 | async-start | bytes 5242880 | tf_op jit(solution)/shard_map/reduce_scatter | solution.py:34
Sparse Core Ops, SparseCore 0:
  28.0 45.4 all-gather.4
  76.8 64.9 all-gather.2
  152.1 88.0 reduce-scatter.1
where the time goes:
time: 247 us
  waiting for transfers between devices  182 us (74%)
  blocking collectives  34.1 us (14%)
  between operations  13.2 us (5%)
  matrix products  10.2 us (4%)
  local copies, waits for them, and re-layouts  5.21 us (2%)
    reduce_scatter x1, waiting for transfers between devices, shards(): lax.psum_scatter(contract(left_band, right_band), 'kpart', scatter_dimens...  88.2 us
    all_gather x1, waiting for transfers between devices, shards(): left_band = lax.all_gather(band_left, 'col', axis=0, tiled=True)  68.3 us
    all_gather x1, waiting for transfers between devices, shards(): right_band = lax.all_gather(band_right, 'row', axis=0, tiled=True)  25.2 us
    all_to_all x1, blocking collectives, shards(): lax.all_to_all(shaped_left, 'row', split_axis=1, concat_axis=3, tiled=True)  17.6 us
    all_to_all x1, blocking collectives, shards(): lax.all_to_all(shaped_right, 'col', split_axis=1, concat_axis=3, tiled=True)  16.5 us
    dot_general x1, matrix products, contract(): lax.dot_general(left_part, right_part, (((0,), (0,)), ((), ())), precisio...  10.2 us
  transfers between devices with their start and end apart: 3, of which 3 were waited for; matrix products, arithmetic and copies ran while one was open for 1% of the time, Pallas kernels for 0%

commit v1 on v0

--- a/solution.py
+++ b/solution.py
@@ -4,6 +4,22 @@
 from jax.sharding import PartitionSpec as P
 
 NB = 64
+
+
+def exchange_in_pairs(shard, axis, split, join):
+    ways, here = (lax.axis_size(axis), lax.axis_index(axis))
+    width = shard.shape[split] // ways
+    shape = list(shard.shape)
+    shape[split] = width
+    height = shape[join]
+    shape[join] = height * ways
+    full = jnp.zeros(shape, shard.dtype)
+    for mask in range(ways):
+        part = lax.dynamic_slice_in_dim(shard, (here ^ mask) * width, width, axis=split)
+        if mask:
+            part = lax.ppermute(part, axis, [(d, d ^ mask) for d in range(ways)])
+        full = lax.dynamic_update_slice_in_dim(full, part, (here ^ mask) * height, axis=join)
+    return full
 
 
 def contract(left_part, right_part):
@@ -22,7 +38,7 @@
     slab_left, local_rows = left_cyclic.shape
     group_left = local_rows // (NB * row_count)
     shaped_left = left_cyclic.reshape(slab_left, row_count, group_left, 1, NB)
-    moved_left = lax.all_to_all(shaped_left, "row", split_axis=1, concat_axis=3, tiled=True)
+    moved_left = exchange_in_pairs(shaped_left, "row", 1, 3)
     band_left = moved_left.reshape(slab_left, local_rows)
     left_band = lax.all_gather(band_left, "col", axis=0, tiled=True)
     slab_right, local_cols = right_cyclic.shape

time: 247 us -> 257 us (1.040)
  starting transfers between devices: 0.09 us -> 30.2 us
  blocking collectives: 34.1 us -> 19.2 us
  waiting for transfers between devices: 182 us -> 177 us
    ppermute x0 -> x7, starting transfers between devices: none -> 30.2 us  [exchange_in_pairs(): part = lax.ppermute(part, axis, [(d, d ^ mask) for d in range(ways)])]
    all_gather x1, waiting for transfers between devices: 68.3 us -> 41.2 us  [shards(): left_band = lax.all_gather(band_left, 'col', axis=0, tiled=True)]
    all_gather x1, waiting for transfers between devices: 25.2 us -> 43.8 us  [shards(): right_band = lax.all_gather(band_right, 'row', axis=0, tiled=True)]
    all_to_all x1 -> x0, blocking collectives: 17.6 us -> none  [shards(): lax.all_to_all(shaped_left, 'row', split_axis=1, concat_axis=3, tiled=True)]
    ppermute x0 -> x7, waiting for transfers between devices: none -> 2.77 us  [exchange_in_pairs(): part = lax.ppermute(part, axis, [(d, d ^ mask) for d in range(ways)])]
    all_to_all x1, blocking collectives: 16.5 us -> 19.2 us  [shards(): lax.all_to_all(shaped_right, 'col', split_axis=1, concat_axis=3, tiled=True)]
  transfers between devices with their start and end apart: 3 -> 10, of which waited for: 3 -> 4; matrix products, arithmetic and copies ran while one was open for 1% -> 2% of each run, Pallas kernels for 0% -> 0%
where the time goes in v1:
time: 257 us
  waiting for transfers between devices  177 us (69%)
  starting transfers between devices  30.2 us (12%)
  blocking collectives  19.2 us (7%)
  between operations  13.4 us (5%)
  matrix products  10.2 us (4%)
  local copies, waits for them, and re-layouts  5.82 us (2%)
    reduce_scatter x1, waiting for transfers between devices, shards(): lax.psum_scatter(contract(left_band, right_band), 'kpart', scatter_dimens...  89.2 us
    all_gather x1, waiting for transfers between devices, shards(): right_band = lax.all_gather(band_right, 'row', axis=0, tiled=True)  43.8 us
    all_gather x1, waiting for transfers between devices, shards(): left_band = lax.all_gather(band_left, 'col', axis=0, tiled=True)  41.2 us
    ppermute x7, starting transfers between devices, exchange_in_pairs(): part = lax.ppermute(part, axis, [(d, d ^ mask) for d in range(ways)])  30.2 us
    all_to_all x1, blocking collectives, shards(): lax.all_to_all(shaped_right, 'col', split_axis=1, concat_axis=3, tiled=True)  19.2 us
    dot_general x1, matrix products, contract(): lax.dot_general(left_part, right_part, (((0,), (0,)), ((), ())), precisio...  10.2 us
  transfers between devices with their start and end apart: 10, of which 4 were waited for; matrix products, arithmetic and copies ran while one was open for 2% of the time, Pallas kernels for 0%

profile of v1, /device:TPU:57, one launch (start us, length us, event | category | flops | bytes accessed | tf_op | source)
XLA Modules:
  0.0 257.1 jit_solution(710982607109292422)
XLA Ops:
  6.5 0.0 copy-start
  6.5 0.0 all-gather.3.cloned.1.call-start
  6.5 1.1 reshape.16
  7.7 0.1 constant_dynamic-slice_fusion
  7.8 5.8 %collective-permute-start.1 = (f32[32,1,2,1,64]{4,3,2,0,1:T(1,128)S(1)}, f32[32,1,2,1,64]{4,3,2,0,1:T(1,128)S(1)}, u32[]{:S(2)}, u32[]{:S(2)}) collective-permute-start(f32[32,1,2,1,64]{4,3,2,0,1:T(1,128)S(1)} %bitcast.31), channel_id=1, source_target_pairs={{0,128},{64,192},{128,0},{192,64},{256,384},{320,448},{384,256},{4... | collective-permute-start | bytes 49160 | tf_op jit(solution)/shard_map/ppermute | solution.py:20
  13.7 4.0 %collective-permute-start = (f32[32,1,2,1,64]{4,3,2,0,1:T(1,128)S(1)}, f32[32,1,2,1,64]{4,3,2,0,1:T(1,128)S(1)}, u32[]{:S(2)}, u32[]{:S(2)}) collective-permute-start(f32[32,1,2,1,64]{4,3,2,0,1:T(1,128)S(1)} %bitcast.30), channel_id=1, source_target_pairs={{0,64},{64,0},{128,192},{192,128},{256,320},{320,256},{384,448},{4... | collective-permute-start | bytes 49160 | tf_op jit(solution)/shard_map/ppermute | solution.py:20
  17.7 6.1 %collective-permute-start.5 = (f32[32,1,2,1,64]{4,3,2,0,1:T(1,128)S(1)}, f32[32,1,2,1,64]{4,3,2,0,1:T(1,128)S(1)}, u32[]{:S(2)}, u32[]{:S(2)}) collective-permute-start(f32[32,1,2,1,64]{4,3,2,0,1:T(1,128)S(1)} %bitcast.26), channel_id=1, source_target_pairs={{0,384},{64,448},{128,256},{192,320},{256,128},{320,192},{384,0},{... | collective-permute-start | bytes 49160 | tf_op jit(solution)/shard_map/ppermute | solution.py:20
  23.8 3.7 %collective-permute-start.3 = (f32[32,1,2,1,64]{4,3,2,0,1:T(1,128)S(1)}, f32[32,1,2,1,64]{4,3,2,0,1:T(1,128)S(1)}, u32[]{:S(2)}, u32[]{:S(2)}) collective-permute-start(f32[32,1,2,1,64]{4,3,2,0,1:T(1,128)S(1)} %bitcast.28), channel_id=1, source_target_pairs={{0,256},{64,320},{128,384},{192,448},{256,0},{320,64},{384,128},{4... | collective-permute-start | bytes 49160 | tf_op jit(solution)/shard_map/ppermute | solution.py:20
  27.5 2.2 collective-permute-start.2
  29.7 0.0 collective-permute-done.1
  29.7 6.4 %collective-permute-start.4 = (f32[32,1,2,1,64]{4,3,2,0,1:T(1,128)S(1)}, f32[32,1,2,1,64]{4,3,2,0,1:T(1,128)S(1)}, u32[]{:S(2)}, u32[]{:S(2)}) collective-permute-start(f32[32,1,2,1,64]{4,3,2,0,1:T(1,128)S(1)} %bitcast.27), channel_id=1, source_target_pairs={{0,320},{64,256},{128,448},{192,384},{256,64},{320,0},{384,192},{4... | collective-permute-start | bytes 49160 | tf_op jit(solution)/shard_map/ppermute | solution.py:20
  36.1 0.0 collective-permute-done
  36.1 1.9 collective-permute-start.6
  38.1 0.2 dynamic_update_slice.24
  38.3 0.2 dynamic_update_slice.25
  38.4 0.2 dynamic_update_slice.26
  38.6 0.0 collective-permute-done.2
  38.6 0.2 dynamic_update_slice.27
  38.7 0.0 collective-permute-done.3
  38.8 0.2 dynamic_update_slice.28
  38.9 0.0 collective-permute-done.4
  38.9 0.2 dynamic_update_slice.29
  39.1 0.0 collective-permute-done.5
  39.1 0.2 dynamic_update_slice.30
  39.3 2.8 %collective-permute-done.6 = f32[32,1,2,1,64]{4,3,2,0,1:T(1,128)S(1)} collective-permute-done((f32[32,1,2,1,64]{4,3,2,0,1:T(1,128)S(1)}, f32[32,1,2,1,64]{4,3,2,0,1:T(1,128)S(1)}, u32[]{:S(2)}, u32[]{:S(2)}) %collective-permute-start.6) | collective-permute-done | bytes 16416 | tf_op jit(solution)/shard_map/ppermute | solution.py:20
  42.0 0.1 dynamic_update_slice.31
  42.2 0.8 reshape.17
  42.9 0.0 all-gather.3.cloned.1.call-update
  43.0 0.0 all-gather.5.cloned.1.call-start
  43.0 0.0 copy-done
  43.0 0.1 reshape.18
  43.2 0.2 copy.38
  43.3 0.3 reshape.20
  43.7 19.2 %all_to_all.4 = f32[16,1,4096]{2,1,0:T(1,128)S(1)} all-to-all(f32[16,1,4096]{2,1,0:T(1,128)S(1)} %reshape.20), channel_id=1, replica_groups=mesh['row'=8,'col'=16,'kpart'=4] {'col'}, dimensions={0} | all-to-all | bytes 524288 | tf_op jit(solution)/shard_map/all_to_all | solution.py:47
  62.9 0.5 broadcast
  63.4 1.3 reduce
  64.7 0.2 reshape.21
  64.9 0.3 copy.28
  65.2 0.9 reshape.19
  66.1 0.0 all-gather.5.cloned.1.call-update
  66.1 0.0 reduce-scatter.2.cloned.1.call-start
  66.2 41.2 %all-gather.3.cloned.1.call-done = f32[512,1024]{1,0:T(8,128)} async-done(((f32[32,1024]{1,0:T(8,128)}), f32[512,1024]{1,0:T(8,128)}) %all-gather.3.cloned.1.call-update) | async-done | bytes 2097168 | tf_op jit(solution)/shard_map/all_gather | solution.py:43
  107.4 43.8 %all-gather.5.cloned.1.call-done = f32[512,1024]{1,0:T(8,128)} async-done(((f32[64,1024]{1,0:T(8,128)}), f32[512,1024]{1,0:T(8,128)}) %all-gather.5.cloned.1.call-update) | async-done | bytes 2097168 | tf_op jit(solution)/shard_map/all_gather | solution.py:49
  151.2 10.2 %fusion = f32[1024,1024]{1,0:T(8,128)} fusion(f32[512,1024]{1,0:T(8,128)} %all-gather.3.cloned.1.call-done, f32[512,1024]{1,0:T(8,128)} %all-gather.5.cloned.1.call-done), kind=kOutput, calls=%fused_computation.9 | convolution fusion | flops 6442450944 | bytes 8388608 | tf_op jit(solution)/shard_map/dot_general | solution.py:26
  161.4 0.0 reduce-scatter.2.cloned.1.call-update
  161.5 89.2 %reduce-scatter.2.cloned.1.call-done = f32[256,1024]{1,0:T(8,128)} async-done(((f32[1024,1024]{1,0:T(8,128)}), f32[256,1024]{1,0:T(8,128)}) %reduce-scatter.2.cloned.1.call-update) | async-done | bytes 1048592 | tf_op jit(solution)/shard_map/reduce_scatter | solution.py:50
  (1 shorter events, 0.0 us)
Async XLA Ops:
  6.5 36.5 %copy-start = (f32[64,1024]{1,0:T(8,128)S(1)}, f32[64,1024]{1,0:T(8,128)}, u32[]{:S(2)}) copy-start(f32[64,1024]{1,0:T(8,128)} %param.3) | copy-start | bytes 786436
  6.5 100.9 %all-gather.3.cloned.1.call-start = ((), (), s32[]{:S(2)}) async-start(), calls=%async_computation.2 | async-start | bytes 2228224 | tf_op jit(solution)/shard_map/all_gather | solution.py:43
  7.8 21.9 %collective-permute-start.1 = (f32[32,1,2,1,64]{4,3,2,0,1:T(1,128)S(1)}, f32[32,1,2,1,64]{4,3,2,0,1:T(1,128)S(1)}, u32[]{:S(2)}, u32[]{:S(2)}) collective-permute-start(f32[32,1,2,1,64]{4,3,2,0,1:T(1,128)S(1)} %bitcast.31), channel_id=1, source_target_pairs={{0,128},{64,192},{128,0},{192,64},{256,384},{320,448},{384,256},{4... | collective-permute-start | bytes 49160 | tf_op jit(solution)/shard_map/ppermute | solution.py:20
  13.7 22.5 %collective-permute-start = (f32[32,1,2,1,64]{4,3,2,0,1:T(1,128)S(1)}, f32[32,1,2,1,64]{4,3,2,0,1:T(1,128)S(1)}, u32[]{:S(2)}, u32[]{:S(2)}) collective-permute-start(f32[32,1,2,1,64]{4,3,2,0,1:T(1,128)S(1)} %bitcast.30), channel_id=1, source_target_pairs={{0,64},{64,0},{128,192},{192,128},{256,320},{320,256},{384,448},{4... | collective-permute-start | bytes 49160 | tf_op jit(solution)/shard_map/ppermute | solution.py:20
  17.7 21.4 %collective-permute-start.5 = (f32[32,1,2,1,64]{4,3,2,0,1:T(1,128)S(1)}, f32[32,1,2,1,64]{4,3,2,0,1:T(1,128)S(1)}, u32[]{:S(2)}, u32[]{:S(2)}) collective-permute-start(f32[32,1,2,1,64]{4,3,2,0,1:T(1,128)S(1)} %bitcast.26), channel_id=1, source_target_pairs={{0,384},{64,448},{128,256},{192,320},{256,128},{320,192},{384,0},{... | collective-permute-start | bytes 49160 | tf_op jit(solution)/shard_map/ppermute | solution.py:20
  23.8 15.0 %collective-permute-start.3 = (f32[32,1,2,1,64]{4,3,2,0,1:T(1,128)S(1)}, f32[32,1,2,1,64]{4,3,2,0,1:T(1,128)S(1)}, u32[]{:S(2)}, u32[]{:S(2)}) collective-permute-start(f32[32,1,2,1,64]{4,3,2,0,1:T(1,128)S(1)} %bitcast.28), channel_id=1, source_target_pairs={{0,256},{64,320},{128,384},{192,448},{256,0},{320,64},{384,128},{4... | collective-permute-start | bytes 49160 | tf_op jit(solution)/shard_map/ppermute | solution.py:20
  27.5 11.0 %collective-permute-start.2 = (f32[32,1,2,1,64]{4,3,2,0,1:T(1,128)S(1)}, f32[32,1,2,1,64]{4,3,2,0,1:T(1,128)S(1)}, u32[]{:S(2)}, u32[]{:S(2)}) collective-permute-start(f32[32,1,2,1,64]{4,3,2,0,1:T(1,128)S(1)} %bitcast.29), channel_id=1, source_target_pairs={{0,192},{64,128},{128,64},{192,0},{256,448},{320,384},{384,320},{4... | collective-permute-start | bytes 49160 | tf_op jit(solution)/shard_map/ppermute | solution.py:20
  29.7 9.2 %collective-permute-start.4 = (f32[32,1,2,1,64]{4,3,2,0,1:T(1,128)S(1)}, f32[32,1,2,1,64]{4,3,2,0,1:T(1,128)S(1)}, u32[]{:S(2)}, u32[]{:S(2)}) collective-permute-start(f32[32,1,2,1,64]{4,3,2,0,1:T(1,128)S(1)} %bitcast.27), channel_id=1, source_target_pairs={{0,320},{64,256},{128,448},{192,384},{256,64},{320,0},{384,192},{4... | collective-permute-start | bytes 49160 | tf_op jit(solution)/shard_map/ppermute | solution.py:20
  36.1 5.9 %collective-permute-start.6 = (f32[32,1,2,1,64]{4,3,2,0,1:T(1,128)S(1)}, f32[32,1,2,1,64]{4,3,2,0,1:T(1,128)S(1)}, u32[]{:S(2)}, u32[]{:S(2)}) collective-permute-start(f32[32,1,2,1,64]{4,3,2,0,1:T(1,128)S(1)} %bitcast.25), channel_id=1, source_target_pairs={{0,448},{64,384},{128,320},{192,256},{256,192},{320,128},{384,64},... | collective-permute-start | bytes 49160 | tf_op jit(solution)/shard_map/ppermute | solution.py:20
  43.0 108.3 %all-gather.5.cloned.1.call-start = ((), (), s32[]{:S(2)}) async-start(), calls=%async_computation.3 | async-start | bytes 2359296 | tf_op jit(solution)/shard_map/all_gather | solution.py:49
  66.1 184.5 %reduce-scatter.2.cloned.1.call-start = ((), (), s32[]{:S(2)}) async-start(), calls=%async_computation.4 | async-start | bytes 5242880 | tf_op jit(solution)/shard_map/reduce_scatter | solution.py:50
Sparse Core Ops, SparseCore 0:
  43.1 64.2 all-gather.2
  109.5 41.7 all-gather.4
  161.6 88.9 reduce-scatter.1
